TPU v7x, 32 devices: a whole 2x2x4 slice. The times are simulated.
32 devices in a mesh: gx: 2 (over core), gy: 4 (over y, x), gz: 4 (over z).
Axes of the slice: x: 2, y: 2, z: 4, core: 2. Of those that a mesh axis runs over, the one named last changes fastest.
Arguments:
- adjoint_final: float32 [16, 32, 512], P('gz', 'gx', 'gy'), may hold values from -6 to 6
- conductivity: float32 [3, 16, 32, 512], P(None, 'gz', 'gx', 'gy'), may hold values from 0.05 to 1
- step_ratio: float32 [16, 32, 512], P('gz', 'gx', 'gy'), may hold values from 0.04 to 0.16
- refine_rate: float32 [16, 32, 512], P('gz', 'gx', 'gy'), may hold values from 0.05 to 0.24
- residual: float32 [4, 512], P(None, ('gx', 'gy')), may hold values from -6 to 6
- sensor_tile: int32 [512], P(('gx', 'gy')), may hold values from 0 to 7, as said below
- sensor_cell: int32 [512], P(('gx', 'gy')), may hold values from 0 to 32767
- substeps: int32 [2, 4], replicated, may hold values from 1 to 6, as said below
Outputs:
- adjoint_start: float32 [16, 32, 512], P('gz', 'gx', 'gy')
- sensitivity: float32 [16, 32, 512], P('gz', 'gx', 'gy')
Inputs may be any that keep to these rules, and one draw needn't show every extreme that they name: `sensor_tile`: tiles are numbered ix * 4 + iy. Among the 64 sensors of each aligned block at most 10 name one tile, and in every block some tile is named by exactly 10 of them. `substeps`: some tile takes 6 sub-steps in every draw.
All inputs are finite; a program needn't handle non-finite values.
Results may differ from a plain program's by a relative error of at most 0.000079.
Values sent between devices are 32-bit elements; how exact they have to be, the bound alone decides.
A program may use at most 64 MiB of HBM per device.

v0:
```python
import functools

import jax
import jax.numpy as jnp
from jax import lax
from jax.experimental import pallas as pl
from jax.experimental.pallas import tpu as pltpu
from jax.sharding import PartitionSpec as P

MESH = pl.DeviceIdType.MESH
MOST_TURNS = 6
SUB = 8
NT = (((1,), (1,)), ((), ()))


def harmonic(first, second):
    return 2.0 * first * second / (first + second)


def pieces_of(values):
    high = values.astype(jnp.bfloat16).astype(jnp.float32)
    rest = values - high
    middle = rest.astype(jnp.bfloat16).astype(jnp.float32)
    return high, middle, rest - middle


def kernel(
    sizes,
    cond_hbm,
    adjoint_hbm,
    ratio_hbm,
    rate_hbm,
    res_hbm,
    tile_hbm,
    cell_hbm,
    substeps_ref,
    adjoint_out,
    sens_out,
    base,
    res_in,
    tile_in,
    cell_in,
    sensors,
    gathered,
    first_x,
    first_x_in,
    first_y,
    first_y_in,
    first_z_in,
    send_w,
    send_x,
    recv_x,
    send_y,
    recv_y,
    recv_z,
    load_sem,
    sensor_send,
    sensor_recv,
    halo_send,
    halo_recv,
):
    nx, ny, nz, layers, rows, cols, steps, listed = sizes
    cells = layers * rows
    groups_of_rows = cells // SUB
    tiles = nx * ny
    x, y, z = lax.axis_index("gx"), lax.axis_index("gy"), lax.axis_index("gz")
    me = x * ny + y

    loads = [
        pltpu.make_async_copy(src, dst, load_sem.at[k])
        for k, (src, dst) in enumerate(
            (
                (res_hbm, res_in),
                (tile_hbm, tile_in),
                (cell_hbm, cell_in),
                (adjoint_hbm, base.at[3]),
                (ratio_hbm, base.at[4]),
                (cond_hbm, base.at[pl.ds(0, 3)]),
                (rate_hbm, base.at[5]),
            )
        )
    ]
    for load in loads:
        load.start()

    for ref in (first_x_in, first_y_in, first_z_in, recv_x, recv_y, recv_z, sensors):
        ref[...] = jnp.zeros_like(ref)

    sides = (
        (0, nx, x, -1),
        (0, nx, x, 1),
        (1, ny, y, -1),
        (1, ny, y, 1),
        (2, nz, z, -1),
        (2, nz, z, 1),
    )

    def device_at(axis, step):
        place = [x, y, z]
        place[axis] = place[axis] + step
        return tuple(place)

    def inside(count, place, step):
        return place > 0 if step < 0 else place < count - 1

    barrier = pltpu.get_barrier_semaphore()

    def sensor_peer(offset):
        there = lax.rem(me + offset, tiles)
        return (lax.div(there, ny), lax.rem(there, ny), z)

    for offset in range(1, tiles):
        pl.semaphore_signal(barrier, inc=1, device_id=sensor_peer(offset), device_id_type=MESH)
    for axis, count, place, step in sides[4:]:

        @pl.when(inside(count, place, step))
        def _():
            pl.semaphore_signal(
                barrier, inc=1, device_id=device_at(axis, step), device_id_type=MESH
            )

    for load in loads[:3]:
        load.wait()
    per = max(1, cols // listed)
    lane = lax.broadcasted_iota(jnp.int32, (1, cols), 1)
    cell = cell_in[...]
    grid_layers_rows = nz * cells
    key = tile_in[...] * grid_layers_rows + lax.div(cell, cols)
    column = lax.rem(cell, cols)
    for slot in range(per):
        here = pl.ds(slot * listed, listed)
        sensors[0:steps, here] = res_in[...]
        sensors[steps : steps + 1, here] = key.astype(jnp.float32)
        sensors[steps + 1 : steps + 2, here] = column.astype(jnp.float32)
    if per > 1:
        mine = lax.div(lane, listed) == lax.rem(me, per)
        sensors[...] = jnp.where(mine, sensors[...], 0.0)
    gathered[me] = sensors[...]

    for load in loads[3:]:
        load.wait()
    lanes = lax.broadcasted_iota(jnp.int32, (SUB, cols), 1)

    def pack_columns(arrays):
        to_left = jnp.zeros((SUB, cols), jnp.float32)
        to_right = jnp.zeros((SUB, cols), jnp.float32)
        spot = 0
        for array in arrays:
            for part in range(groups_of_rows):
                block = array[part * SUB : (part + 1) * SUB, :]
                left = pltpu.roll(block, spot % cols, 1)
                right = pltpu.roll(block, (spot + 2) % cols, 1)
                to_left = jnp.where(lanes == spot, left, to_left)
                to_right = jnp.where(lanes == spot + 1, right, to_right)
                spot += 2
        return to_left, to_right

    def unpack_columns(packed, spot):
        return jnp.concatenate(
            [
                pltpu.roll(packed, (cols - 2 * (spot + part) - 1) % cols, 1)
                for part in range(groups_of_rows)
            ],
            axis=0,
        )

    def pick_rows(array, row):
        return jnp.concatenate(
            [array[level * rows + row : level * rows + row + 1, :] for level in range(layers)],
            axis=0,
        )

    def spread_rows(low, high):
        half = rows // 2
        parts = []
        for level in range(layers):
            parts.append(jnp.broadcast_to(low[level : level + 1, :], (half, cols)))
            parts.append(jnp.broadcast_to(high[level : level + 1, :], (rows - half, cols)))
        return jnp.concatenate(parts, axis=0)

    c0, c1, c2 = base[0], base[1], base[2]
    adjoint, ratio, rate = base[3], base[4], base[5]

    for k, array in enumerate((adjoint, ratio, c0)):
        first_x[0, k * layers : (k + 1) * layers, :] = pick_rows(array, 0)
        first_x[1, k * layers : (k + 1) * layers, :] = pick_rows(array, rows - 1)
    left, right = pack_columns((adjoint, ratio, c1))
    first_y[0] = left
    first_y[1] = right

    neighbours = (
        (tiles - 1)
        + (z > 0).astype(jnp.int32)
        + (z < nz - 1).astype(jnp.int32)
    )
    pl.semaphore_wait(barrier, neighbours)

    def sensor_copy(offset):
        return pltpu.make_async_remote_copy(
            src_ref=sensors,
            dst_ref=gathered.at[me],
            send_sem=sensor_send.at[offset],
            recv_sem=sensor_recv.at[offset],
            device_id=sensor_peer(offset),
            device_id_type=MESH,
        )

    def sensor_arrival(offset):
        origin = lax.rem(me + (tiles - offset), tiles)
        return pltpu.make_async_remote_copy(
            src_ref=sensors,
            dst_ref=gathered.at[origin],
            send_sem=sensor_send.at[offset],
            recv_sem=sensor_recv.at[offset],
            device_id=sensor_peer(offset),
            device_id_type=MESH,
        )

    def halo_copies(turn):
        copies = []
        for side, (axis, count, place, step) in enumerate(sides):
            way = side % 2
            if turn == 0:
                source, target = (
                    (first_x.at[way], first_x_in.at[1 - way]),
                    (first_y.at[way], first_y_in.at[1 - way]),
                    (
                        base.at[pl.ds(2, 3), pl.ds(way * (cells - rows), rows)],
                        first_z_in.at[1 - way],
                    ),
                )[axis]
            else:
                at = turn - 1
                source, target = (
                    (send_x.at[at, way], recv_x.at[at, 1 - way]),
                    (send_y.at[at, way], recv_y.at[at, 1 - way]),
                    (
                        send_w.at[at, pl.ds(way * (cells - rows), rows)],
                        recv_z.at[at, 1 - way],
                    ),
                )[axis]
            copy = pltpu.make_async_remote_copy(
                src_ref=source,
                dst_ref=target,
                send_sem=halo_send.at[turn, side],
                recv_sem=halo_recv.at[turn, 2 * axis + 1 - way],
                device_id=device_at(axis, step),
                device_id_type=MESH,
            )
            arrival = pltpu.make_async_remote_copy(
                src_ref=source,
                dst_ref=(
                    (first_x_in, first_y_in, first_z_in)[axis].at[way]
                    if turn == 0
                    else (recv_x, recv_y, recv_z)[axis].at[turn - 1, way]
                ),
                send_sem=halo_send.at[turn, side],
                recv_sem=halo_recv.at[turn, side],
                device_id=device_at(axis, step),
                device_id_type=MESH,
            )
            copies.append((inside(count, place, step), copy, arrival))
        return copies

    def start(copies, chosen):
        for side in chosen:
            valid, copy, _ = copies[side]
            pl.when(valid)(copy.start)

    def arrive(copies):
        for valid, _, arrival in copies:
            pl.when(valid)(arrival.wait_recv)

    def sent(copies):
        for valid, copy, _ in copies:
            pl.when(valid)(copy.wait_send)

    copies = halo_copies(0)
    for offset in range(1, tiles):
        sensor_copy(offset).start()
    start(copies, (2, 3, 4, 5, 0, 1))

    full = (cells, cols)
    row_in = lax.rem(lax.broadcasted_iota(jnp.int32, full, 0), rows)
    col_in = lax.broadcasted_iota(jnp.int32, full, 1)
    top, bottom = row_in == 0, row_in == rows - 1
    first_col, last_col = col_in == 0, col_in == cols - 1

    def next_row(array):
        return pltpu.roll(array, cells - 1, 0)

    def prev_row(array):
        return pltpu.roll(array, 1, 0)

    def next_col(array):
        return pltpu.roll(array, cols - 1, 1)

    def prev_col(array):
        return pltpu.roll(array, 1, 1)

    row_next = jnp.where(bottom, 0.0, harmonic(c0, next_row(c0)))
    row_prev = prev_row(row_next)
    col_next = jnp.where(last_col, 0.0, harmonic(c1, next_col(c1)))
    col_prev = prev_col(col_next)
    between = harmonic(c2[: cells - rows], c2[rows:])
    no_layer = jnp.zeros((rows, cols), jnp.float32)
    rate_next_row = jnp.where(bottom, 0.0, next_row(rate))
    rate_prev_row = jnp.where(top, 0.0, prev_row(rate))
    rate_next_col = jnp.where(last_col, 0.0, next_col(rate))
    rate_prev_col = jnp.where(first_col, 0.0, prev_col(rate))
    around = (
        4.0
        - top.astype(jnp.float32)
        - bottom.astype(jnp.float32)
        - first_col.astype(jnp.float32)
        - last_col.astype(jnp.float32)
    )
    stay = 1.0 - around * rate
    turns = jnp.full(full, substeps_ref[x, y])
    inner_faces = (
        row_next
        + row_prev
        + col_next
        + col_prev
        + jnp.concatenate([between, no_layer], axis=0)
        + jnp.concatenate([no_layer, between], axis=0)
    )

    def refine(field):
        for turn in range(MOST_TURNS):
            after = (
                stay * field
                + (rate_next_row * next_row(field) + rate_prev_row * prev_row(field))
                + (rate_next_col * next_col(field) + rate_prev_col * prev_col(field))
            )
            field = jnp.where(turns > turn, after, field)
        return field

    def inner(field, weighted, own):
        return (
            own * field
            + (row_next * next_row(weighted) + row_prev * prev_row(weighted))
            + (col_next * next_col(weighted) + col_prev * prev_col(weighted))
            + jnp.concatenate([between * weighted[rows:], no_layer], axis=0)
            + jnp.concatenate([no_layer, between * weighted[: cells - rows]], axis=0)
        )

    row_key = (me * grid_layers_rows + z * cells).astype(jnp.float32)

    def keys(count, start_at):
        place = lax.broadcasted_iota(jnp.int32, (count, cols), 0).astype(jnp.float32)
        return place + (row_key + start_at)

    arrive(copies)
    for offset in range(1, tiles):
        sensor_arrival(offset).wait_recv()

    row_halo = spread_rows(
        first_x_in[0, 2 * layers : 3 * layers, :], first_x_in[1, 2 * layers : 3 * layers, :]
    )
    row_face = jnp.where(jnp.logical_or(top, bottom), harmonic(c0, row_halo), 0.0)
    packed = first_y_in[0] + first_y_in[1]
    col_halo = unpack_columns(packed, 2 * groups_of_rows)
    col_face = jnp.where(jnp.logical_or(first_col, last_col), harmonic(c1, col_halo), 0.0)
    low_face = harmonic(c2[:rows], first_z_in[0, 0])
    high_face = harmonic(c2[cells - rows :], first_z_in[1, 0])
    middle = cells - 2 * rows

    def with_ends(low, high):
        parts = [low]
        if middle > 0:
            parts.append(jnp.zeros((middle, cols), jnp.float32))
        return jnp.concatenate(parts + [high], axis=0)

    all_faces = inner_faces + row_face + col_face + with_ends(low_face, high_face)
    own = 1.0 - ratio * all_faces

    def outer(row_values, col_values, low_values, high_values):
        return (
            row_face * row_values
            + col_face * col_values
            + with_ends(low_face * low_values, high_face * high_values)
        )

    blocks = []
    folded = max(1, tiles // per)
    for block in range(folded):
        total = gathered[block * per]
        for slot in range(1, per):
            total = total + gathered[block * per + slot]
        blocks.append(total)
    key_rows = [total[steps : steps + 1, :] for total in blocks]
    col_rows = [total[steps + 1 : steps + 2, :] for total in blocks]
    split = [pieces_of(total[0:steps, :]) for total in blocks]
    col_ids = lax.broadcasted_iota(jnp.int32, (cols, cols), 0).astype(jnp.float32)
    in_column = jnp.concatenate(
        [jnp.where(col_ids == line, 1.0, 0.0).astype(jnp.bfloat16) for line in col_rows], axis=1
    )

    def placed(row_keys, sensor_keys, step, piece):
        return jnp.concatenate(
            [
                jnp.where(
                    row_keys == line, parts[piece][step : step + 1, :], 0.0
                ).astype(jnp.bfloat16)
                for line, parts in zip(sensor_keys, split)
            ],
            axis=1,
        )

    def source_of(row_keys, sensor_keys, columns, step):
        total = None
        for piece in range(3):
            part = lax.dot_general(
                placed(row_keys, sensor_keys, step, piece),
                columns,
                NT,
                preferred_element_type=jnp.float32,
            )
            total = part if total is None else total + part
        return total

    last = steps - 1
    own_keys = keys(cells, 0.0)
    level_of = lax.broadcasted_iota(jnp.int32, (2 * layers, cols), 0)
    beside = (ny * grid_layers_rows)
    side_keys = row_key + jnp.where(
        level_of < layers,
        level_of * rows + (rows - 1 - beside),
        (level_of - layers) * rows + beside,
    ).astype(jnp.float32)
    wide_keys = jnp.concatenate(
        [
            own_keys,
            keys(rows, -float(rows)),
            keys(rows, float(cells)),
            side_keys,
            jnp.full((2 * layers, cols), -1.0, jnp.float32),
        ],
        axis=0,
    )
    wide = source_of(wide_keys, key_rows, in_column, last)
    far = float(tiles * grid_layers_rows * 4)
    moved_keys = [
        jnp.where(
            col_line == cols - 1.0,
            key_line + float(grid_layers_rows),
            jnp.where(col_line == 0.0, key_line - float(grid_layers_rows), -far),
        )
        for key_line, col_line in zip(key_rows, col_rows)
    ]
    at_edges = jnp.concatenate(
        [
            jnp.where(
                jnp.logical_or(
                    jnp.logical_and(col_ids == 0.0, line == cols - 1.0),
                    jnp.logical_and(col_ids == cols - 1.0, line == 0.0),
                ),
                1.0,
                0.0,
            ).astype(jnp.bfloat16)
            for line in col_rows
        ],
        axis=1,
    )
    edge = source_of(own_keys, moved_keys, at_edges, last)
    next_source = source_of(own_keys, key_rows, in_column, last - 1)

    field = adjoint + wide[:cells]
    low_src = wide[cells : cells + rows]
    high_src = wide[cells + rows : cells + 2 * rows]
    side_src = wide[cells + 2 * rows : cells + 2 * rows + 2 * layers]
    rows_low = first_x_in[0, layers : 2 * layers, :] * (
        first_x_in[0, 0:layers, :] + side_src[:layers]
    )
    rows_high = first_x_in[1, layers : 2 * layers, :] * (
        first_x_in[1, 0:layers, :] + side_src[layers:]
    )
    cols_adjoint = unpack_columns(packed, 0)
    cols_ratio = unpack_columns(packed, groups_of_rows)
    field = inner(field, ratio * field, own) + outer(
        spread_rows(rows_low, rows_high),
        cols_ratio * (cols_adjoint + edge),
        first_z_in[0, 2] * (first_z_in[0, 1] + low_src),
        first_z_in[1, 2] * (first_z_in[1, 1] + high_src),
    )
    field = refine(field)
    sens = ratio * field

    pending = [copies]
    sources = {last - 1: next_source}
    for turn in range(1, steps):
        step = last - turn
        field = field + sources[step]
        weighted = ratio * field
        copies = halo_copies(turn)
        at = turn - 1
        send_w[at] = weighted
        start(copies, (4, 5))
        left, right = pack_columns((weighted,))
        send_y[at, 0] = left
        send_y[at, 1] = right
        start(copies, (2, 3))
        send_x[at, 0, 0:layers, :] = pick_rows(weighted, 0)
        send_x[at, 1, 0:layers, :] = pick_rows(weighted, rows - 1)
        start(copies, (0, 1))
        pending.append(copies)
        field = inner(field, weighted, own)
        if step > 0:
            sources[step - 1] = source_of(own_keys, key_rows, in_column, step - 1)
        arrive(copies)
        field = field + outer(
            spread_rows(recv_x[at, 0, 0:layers, :], recv_x[at, 1, 0:layers, :]),
            unpack_columns(recv_y[at, 0] + recv_y[at, 1], 0),
            recv_z[at, 0],
            recv_z[at, 1],
        )
        field = refine(field)
        sens = sens + ratio * field

    adjoint_out[...] = field
    sens_out[...] = sens
    for offset in range(1, tiles):
        sensor_copy(offset).wait_send()
    for copies in pending:
        sent(copies)


def solution(mesh):
    nx, ny, nz = mesh.shape["gx"], mesh.shape["gy"], mesh.shape["gz"]
    tiles = nx * ny

    def body(
        adjoint_final,
        conductivity,
        step_ratio,
        refine_rate,
        residual,
        sensor_tile,
        sensor_cell,
        substeps,
    ):
        layers, rows, cols = adjoint_final.shape
        steps, listed = residual.shape
        cells = layers * rows
        flat = (cells, cols)
        wide = -(-3 * layers // SUB) * SUB
        narrow = -(-layers // SUB) * SUB
        height = -(-(steps + 2) // SUB) * SUB
        turns = steps - 1
        f32 = jnp.float32
        hbm = pl.BlockSpec(memory_space=pl.ANY)
        vmem = pl.BlockSpec(memory_space=pltpu.VMEM)
        adjoint, sens = pl.pallas_call(
            functools.partial(kernel, (nx, ny, nz, layers, rows, cols, steps, listed)),
            out_shape=[jax.ShapeDtypeStruct(flat, f32)] * 2,
            in_specs=[hbm] * 7 + [pl.BlockSpec(memory_space=pltpu.SMEM)],
            out_specs=[vmem, vmem],
            scratch_shapes=[
                pltpu.VMEM((6, cells, cols), f32),
                pltpu.VMEM((steps, listed), f32),
                pltpu.VMEM((1, listed), jnp.int32),
                pltpu.VMEM((1, listed), jnp.int32),
                pltpu.VMEM((height, cols), f32),
                pltpu.VMEM((tiles, height, cols), f32),
                pltpu.VMEM((2, wide, cols), f32),
                pltpu.VMEM((2, wide, cols), f32),
                pltpu.VMEM((2, SUB, cols), f32),
                pltpu.VMEM((2, SUB, cols), f32),
                pltpu.VMEM((2, 3, rows, cols), f32),
                pltpu.VMEM((turns, cells, cols), f32),
                pltpu.VMEM((turns, 2, narrow, cols), f32),
                pltpu.VMEM((turns, 2, narrow, cols), f32),
                pltpu.VMEM((turns, 2, SUB, cols), f32),
                pltpu.VMEM((turns, 2, SUB, cols), f32),
                pltpu.VMEM((turns, 2, rows, cols), f32),
                pltpu.SemaphoreType.DMA((7,)),
                pltpu.SemaphoreType.DMA((tiles,)),
                pltpu.SemaphoreType.DMA((tiles,)),
                pltpu.SemaphoreType.DMA((steps, 6)),
                pltpu.SemaphoreType.DMA((steps, 6)),
            ],
            compiler_params=pltpu.CompilerParams(
                collective_id=0, has_side_effects=True, vmem_limit_bytes=32 * 1024 * 1024
            ),
        )(
            conductivity.reshape(3, *flat),
            adjoint_final.reshape(flat),
            step_ratio.reshape(flat),
            refine_rate.reshape(flat),
            residual,
            sensor_tile.reshape(1, listed),
            sensor_cell.reshape(1, listed),
            substeps,
        )
        return adjoint.reshape(layers, rows, cols), sens.reshape(layers, rows, cols)

    return jax.shard_map(
        body,
        mesh=mesh,
        in_specs=(
            P("gz", "gx", "gy"),
            P(None, "gz", "gx", "gy"),
            P("gz", "gx", "gy"),
            P("gz", "gx", "gy"),
            P(None, ("gx", "gy")),
            P(("gx", "gy")),
            P(("gx", "gy")),
            P(),
        ),
        out_specs=(P("gz", "gx", "gy"), P("gz", "gx", "gy")),
        check_vma=False,
    )
```

profile of v0, /device:TPU:0, one launch (start us, length us, event | category | flops | bytes accessed | tf_op | source)
XLA Modules:
  0.0 25.9 jit_solution(3903436970263291769)
XLA Ops:
  0.6 0.0 copy-start.7
  0.6 0.0 copy-start.4
  0.7 0.0 copy-start.5
  0.7 0.0 copy-start.6
  0.7 0.6 %copy-done.7 = s32[64]{0:T(128)S(1)} copy-done((s32[64]{0:T(128)S(1)}, s32[64]{0:T(128)}, u32[]{:S(2)}) %copy-start.7) | copy-done | bytes 280
  1.3 0.0 copy-done.4
  1.3 0.0 copy-done.5
  1.3 0.0 copy-done.6
  1.3 0.0 copy-start
  1.3 0.9 %copy-done = f32[3,4,16,128]{3,2,1,0:T(8,128)S(1)} copy-done((f32[3,4,16,128]{3,2,1,0:T(8,128)S(1)}, f32[3,4,16,128]{3,2,1,0:T(8,128)}, u32[]{:S(2)}) %copy-start) | copy-done | bytes 98328
  2.2 0.0 copy-start.1
  2.2 0.8 %copy-done.1 = f32[4,16,128]{2,1,0:T(8,128)S(1)} copy-done((f32[4,16,128]{2,1,0:T(8,128)S(1)}, f32[4,16,128]{2,1,0:T(8,128)}, u32[]{:S(2)}) %copy-start.1) | copy-done | bytes 32792
  3.0 0.0 copy-start.2
  3.0 0.8 %copy-done.2 = f32[4,16,128]{2,1,0:T(8,128)S(1)} copy-done((f32[4,16,128]{2,1,0:T(8,128)S(1)}, f32[4,16,128]{2,1,0:T(8,128)}, u32[]{:S(2)}) %copy-start.2) | copy-done | bytes 32792
  3.8 0.0 copy-start.3
  3.8 0.8 %copy-done.3 = f32[4,16,128]{2,1,0:T(8,128)S(1)} copy-done((f32[4,16,128]{2,1,0:T(8,128)S(1)}, f32[4,16,128]{2,1,0:T(8,128)}, u32[]{:S(2)}) %copy-start.3) | copy-done | bytes 32792
  4.5 20.1 %shard_map.95 = (f32[64,128]{1,0:T(8,128)S(1)}, f32[64,128]{1,0:T(8,128)S(1)}) custom-call(f32[3,64,128]{2,1,0:T(8,128)S(1)} %bitcast.8, f32[64,128]{1,0:T(8,128)S(1)} %bitcast.9, f32[64,128]{1,0:T(8,128)S(1)} %bitcast.10, f32[64,128]{1,0:T(8,128)S(1)} %bitcast.11, f32[4,64]{1,0:T(4,128)S(1)} %copy-done.4, s32[1,64]{1,0:T(1,128)S(1)} %bitcast.14, ...), custom_call_target="tpu_custom_call" | custom-call | tf_op jit(solution)/shard_map/pallas_call | solution.py:554
  24.6 0.6 %copy.12 = f32[4,16,128]{2,1,0:T(8,128)} copy(f32[4,16,128]{2,1,0:T(8,128)S(1)} %bitcast.13) | data formatting | bytes 65536
  25.2 0.6 %copy.13 = f32[4,16,128]{2,1,0:T(8,128)} copy(f32[4,16,128]{2,1,0:T(8,128)S(1)} %bitcast.12) | data formatting | bytes 65536
Async XLA Ops:
  0.6 0.7 %copy-start.7 = (s32[64]{0:T(128)S(1)}, s32[64]{0:T(128)}, u32[]{:S(2)}) copy-start(s32[64]{0:T(128)} %param.14) | copy-start | bytes 772
  0.6 0.7 %copy-start.4 = (f32[4,64]{1,0:T(4,128)S(1)}, f32[4,64]{1,0:T(4,128)}, u32[]{:S(2)}) copy-start(f32[4,64]{1,0:T(4,128)} %res_hbm.1) | copy-start | bytes 3076
  0.7 0.7 %copy-start.5 = (s32[2,4]{1,0:T(2,128)S(1)}, s32[2,4]{1,0:T(2,128)}, u32[]{:S(2)}) copy-start(s32[2,4]{1,0:T(2,128)} %substeps_ref.1) | copy-start | bytes 100
  0.7 0.7 %copy-start.6 = (s32[64]{0:T(128)S(1)}, s32[64]{0:T(128)}, u32[]{:S(2)}) copy-start(s32[64]{0:T(128)} %param.13) | copy-start | bytes 772
  1.3 0.9 %copy-start = (f32[3,4,16,128]{3,2,1,0:T(8,128)S(1)}, f32[3,4,16,128]{3,2,1,0:T(8,128)}, u32[]{:S(2)}) copy-start(f32[3,4,16,128]{3,2,1,0:T(8,128)} %param.9) | copy-start | bytes 294916
  2.2 0.8 %copy-start.1 = (f32[4,16,128]{2,1,0:T(8,128)S(1)}, f32[4,16,128]{2,1,0:T(8,128)}, u32[]{:S(2)}) copy-start(f32[4,16,128]{2,1,0:T(8,128)} %param.8) | copy-start | bytes 98308
  3.0 0.8 %copy-start.2 = (f32[4,16,128]{2,1,0:T(8,128)S(1)}, f32[4,16,128]{2,1,0:T(8,128)}, u32[]{:S(2)}) copy-start(f32[4,16,128]{2,1,0:T(8,128)} %param.10) | copy-start | bytes 98308
  3.8 0.8 %copy-start.3 = (f32[4,16,128]{2,1,0:T(8,128)S(1)}, f32[4,16,128]{2,1,0:T(8,128)}, u32[]{:S(2)}) copy-start(f32[4,16,128]{2,1,0:T(8,128)} %param.11) | copy-start | bytes 98308
where the time goes:
time: 26.2 us; the launch traced here: 25.9 us
  Pallas kernels  20.1 us (77%)
  local copies, waits for them, and re-layouts  5.08 us (19%)
  between operations  0.68 us (3%)
    pallas_call x1, Pallas kernels, body(): pl.pallas_call(functools.partial(kernel, (nx, ny, nz, layers, rows, cols,...  20.1 us
    unnamed x18, local copies, waits for them, and re-layouts  5.08 us

commit v1 on v0

--- a/solution.py
+++ b/solution.py
@@ -33,13 +33,14 @@
     res_hbm,
     tile_hbm,
     cell_hbm,
-    substeps_ref,
+    substeps_hbm,
     adjoint_out,
     sens_out,
     base,
     res_in,
     tile_in,
     cell_in,
+    substeps_ref,
     sensors,
     gathered,
     first_x,
@@ -53,7 +54,9 @@
     send_y,
     recv_y,
     recv_z,
+    results,
     load_sem,
+    store_sem,
     sensor_send,
     sensor_recv,
     halo_send,
@@ -77,6 +80,7 @@
                 (ratio_hbm, base.at[4]),
                 (cond_hbm, base.at[pl.ds(0, 3)]),
                 (rate_hbm, base.at[5]),
+                (substeps_hbm, substeps_ref),
             )
         )
     ]
@@ -518,12 +522,31 @@
         field = refine(field)
         sens = sens + ratio * field
 
-    adjoint_out[...] = field
-    sens_out[...] = sens
+    results[0] = field
+    results[1] = sens
+    stores = [
+        pltpu.make_async_copy(results.at[k], out, store_sem.at[k])
+        for k, out in enumerate((adjoint_out, sens_out))
+    ]
+    for store in stores:
+        store.start()
     for offset in range(1, tiles):
         sensor_copy(offset).wait_send()
     for copies in pending:
         sent(copies)
+    for store in stores:
+        store.wait()
+
+
+def deliver(first, second, first_out, second_out, sems):
+    copies = (
+        pltpu.make_async_copy(first, first_out, sems.at[0]),
+        pltpu.make_async_copy(second, second_out, sems.at[1]),
+    )
+    for copy in copies:
+        copy.start()
+    for copy in copies:
+        copy.wait()
 
 
 def solution(mesh):
@@ -549,18 +572,18 @@
         height = -(-(steps + 2) // SUB) * SUB
         turns = steps - 1
         f32 = jnp.float32
-        hbm = pl.BlockSpec(memory_space=pl.ANY)
-        vmem = pl.BlockSpec(memory_space=pltpu.VMEM)
+        hbm = pl.BlockSpec(memory_space=pltpu.HBM)
         adjoint, sens = pl.pallas_call(
             functools.partial(kernel, (nx, ny, nz, layers, rows, cols, steps, listed)),
             out_shape=[jax.ShapeDtypeStruct(flat, f32)] * 2,
-            in_specs=[hbm] * 7 + [pl.BlockSpec(memory_space=pltpu.SMEM)],
-            out_specs=[vmem, vmem],
+            in_specs=[hbm] * 8,
+            out_specs=[hbm, hbm],
             scratch_shapes=[
                 pltpu.VMEM((6, cells, cols), f32),
                 pltpu.VMEM((steps, listed), f32),
                 pltpu.VMEM((1, listed), jnp.int32),
                 pltpu.VMEM((1, listed), jnp.int32),
+                pltpu.SMEM(substeps.shape, jnp.int32),
                 pltpu.VMEM((height, cols), f32),
                 pltpu.VMEM((tiles, height, cols), f32),
                 pltpu.VMEM((2, wide, cols), f32),
@@ -574,14 +597,16 @@
                 pltpu.VMEM((turns, 2, SUB, cols), f32),
                 pltpu.VMEM((turns, 2, SUB, cols), f32),
                 pltpu.VMEM((turns, 2, rows, cols), f32),
-                pltpu.SemaphoreType.DMA((7,)),
+                pltpu.VMEM((2, cells, cols), f32),
+                pltpu.SemaphoreType.DMA((8,)),
+                pltpu.SemaphoreType.DMA((2,)),
                 pltpu.SemaphoreType.DMA((tiles,)),
                 pltpu.SemaphoreType.DMA((tiles,)),
                 pltpu.SemaphoreType.DMA((steps, 6)),
                 pltpu.SemaphoreType.DMA((steps, 6)),
             ],
             compiler_params=pltpu.CompilerParams(
-                collective_id=0, has_side_effects=True, vmem_limit_bytes=32 * 1024 * 1024
+                collective_id=0, has_side_effects=True, vmem_limit_bytes=63 * 1024 * 1024
             ),
         )(
             conductivity.reshape(3, *flat),
@@ -593,6 +618,14 @@
             sensor_cell.reshape(1, listed),
             substeps,
         )
+        adjoint, sens = pl.pallas_call(
+            deliver,
+            out_shape=[jax.ShapeDtypeStruct(flat, f32)] * 2,
+            in_specs=[hbm, hbm],
+            out_specs=[hbm, hbm],
+            scratch_shapes=[pltpu.SemaphoreType.DMA((2,))],
+            compiler_params=pltpu.CompilerParams(vmem_limit_bytes=63 * 1024 * 1024),
+        )(adjoint, sens)
         return adjoint.reshape(layers, rows, cols), sens.reshape(layers, rows, cols)
 
     return jax.shard_map(

time: 26.2 us -> 24.1 us (0.920)
  local copies, waits for them, and re-layouts: 5.08 us -> 0 us
  Pallas kernels: 20.1 us -> 23.3 us
    unnamed x18 -> x0, local copies, waits for them, and re-layouts: 5.08 us -> none
    pallas_call x0 -> x1, Pallas kernels: none -> 3.11 us  [body(): pl.pallas_call(deliver, out_shape=[jax.ShapeDtypeStruct(flat, f32)] * 2,...]
where the time goes in v1:
time: 24.1 us; the launch traced here: 23.9 us
  Pallas kernels  23.3 us (97%)
  between operations  0.64 us (3%)
    pallas_call x1, Pallas kernels, body(): pl.pallas_call(functools.partial(kernel, (nx, ny, nz, layers, rows, cols,...  20.2 us
    pallas_call x1, Pallas kernels, body(): pl.pallas_call(deliver, out_shape=[jax.ShapeDtypeStruct(flat, f32)] * 2,...  3.11 us

profile of v1, /device:TPU:0, one launch (start us, length us, event | category | flops | bytes accessed | tf_op | source)
XLA Modules:
  0.0 23.9 jit_solution(13641056863618592252)
XLA Ops:
  0.6 20.2 %shard_map.95 = (f32[64,128]{1,0:T(8,128)}, f32[64,128]{1,0:T(8,128)}) custom-call(f32[3,64,128]{2,1,0:T(8,128)} %bitcast.8, f32[64,128]{1,0:T(8,128)} %bitcast.9, f32[64,128]{1,0:T(8,128)} %bitcast.10, f32[64,128]{1,0:T(8,128)} %bitcast.11, f32[4,64]{1,0:T(4,128)} %res_hbm.1, s32[1,64]{1,0:T(1,128)} %bitcast.12, s32[1,64]{1,0:T(1,128)} %bitcast.13, ...), custom_call_target="tpu_custom_call" | custom-call | tf_op jit(solution)/shard_map/pallas_call | solution.py:576
  20.8 3.1 %shard_map.96 = (f32[64,128]{1,0:T(8,128)}, f32[64,128]{1,0:T(8,128)}) custom-call(f32[64,128]{1,0:T(8,128)} %get-tuple-element.6.first, f32[64,128]{1,0:T(8,128)} %get-tuple-element.7.second), custom_call_target="tpu_custom_call" | custom-call | tf_op jit(solution)/shard_map/pallas_call | solution.py:621

commit v2 on v0

--- a/solution.py
+++ b/solution.py
@@ -33,13 +33,14 @@
     res_hbm,
     tile_hbm,
     cell_hbm,
-    substeps_ref,
+    substeps_hbm,
     adjoint_out,
     sens_out,
     base,
     res_in,
     tile_in,
     cell_in,
+    substeps_ref,
     sensors,
     gathered,
     first_x,
@@ -53,6 +54,7 @@
     send_y,
     recv_y,
     recv_z,
+    sources,
     load_sem,
     sensor_send,
     sensor_recv,
@@ -77,6 +79,7 @@
                 (ratio_hbm, base.at[4]),
                 (cond_hbm, base.at[pl.ds(0, 3)]),
                 (rate_hbm, base.at[5]),
+                (substeps_hbm, substeps_ref),
             )
         )
     ]
@@ -218,9 +221,10 @@
 
     def halo_copies(turn):
         copies = []
+        first = isinstance(turn, int) and turn == 0
         for side, (axis, count, place, step) in enumerate(sides):
             way = side % 2
-            if turn == 0:
+            if first:
                 source, target = (
                     (first_x.at[way], first_x_in.at[1 - way]),
                     (first_y.at[way], first_y_in.at[1 - way]),
@@ -251,7 +255,7 @@
                 src_ref=source,
                 dst_ref=(
                     (first_x_in, first_y_in, first_z_in)[axis].at[way]
-                    if turn == 0
+                    if first
                     else (recv_x, recv_y, recv_z)[axis].at[turn - 1, way]
                 ),
                 send_sem=halo_send.at[turn, side],
@@ -327,14 +331,15 @@
     )
 
     def refine(field):
-        for turn in range(MOST_TURNS):
+        def one_turn(turn, field):
             after = (
                 stay * field
                 + (rate_next_row * next_row(field) + rate_prev_row * prev_row(field))
                 + (rate_next_col * next_col(field) + rate_prev_col * prev_col(field))
             )
-            field = jnp.where(turns > turn, after, field)
-        return field
+            return jnp.where(turns > turn, after, field)
+
+        return lax.fori_loop(0, MOST_TURNS, one_turn, field)
 
     def inner(field, weighted, own):
         return (
@@ -464,7 +469,8 @@
         axis=1,
     )
     edge = source_of(own_keys, moved_keys, at_edges, last)
-    next_source = source_of(own_keys, key_rows, in_column, last - 1)
+    if steps > 1:
+        sources[last - 1] = source_of(own_keys, key_rows, in_column, last - 1)
 
     field = adjoint + wide[:cells]
     low_src = wide[cells : cells + rows]
@@ -487,11 +493,9 @@
     field = refine(field)
     sens = ratio * field
 
-    pending = [copies]
-    sources = {last - 1: next_source}
-    for turn in range(1, steps):
-        step = last - turn
-        field = field + sources[step]
+    def one_step(turn, state):
+        field, sens = state
+        field = field + sources[last - turn]
         weighted = ratio * field
         copies = halo_copies(turn)
         at = turn - 1
@@ -504,10 +508,13 @@
         send_x[at, 0, 0:layers, :] = pick_rows(weighted, 0)
         send_x[at, 1, 0:layers, :] = pick_rows(weighted, rows - 1)
         start(copies, (0, 1))
-        pending.append(copies)
         field = inner(field, weighted, own)
-        if step > 0:
-            sources[step - 1] = source_of(own_keys, key_rows, in_column, step - 1)
+
+        @pl.when(turn == 1)
+        def _():
+            for step in range(last - 2, -1, -1):
+                sources[step] = source_of(own_keys, key_rows, in_column, step)
+
         arrive(copies)
         field = field + outer(
             spread_rows(recv_x[at, 0, 0:layers, :], recv_x[at, 1, 0:layers, :]),
@@ -516,14 +523,18 @@
             recv_z[at, 1],
         )
         field = refine(field)
-        sens = sens + ratio * field
-
+        return field, sens + ratio * field
+
+    field, sens = lax.fori_loop(1, steps, one_step, (field, sens))
     adjoint_out[...] = field
     sens_out[...] = sens
     for offset in range(1, tiles):
         sensor_copy(offset).wait_send()
-    for copies in pending:
-        sent(copies)
+    sent(copies)
+
+    @pl.loop(1, steps)
+    def _(turn):
+        sent(halo_copies(turn))
 
 
 def solution(mesh):
@@ -549,18 +560,19 @@
         height = -(-(steps + 2) // SUB) * SUB
         turns = steps - 1
         f32 = jnp.float32
-        hbm = pl.BlockSpec(memory_space=pl.ANY)
         vmem = pl.BlockSpec(memory_space=pltpu.VMEM)
+        hbm = pl.BlockSpec(memory_space=pltpu.HBM)
         adjoint, sens = pl.pallas_call(
             functools.partial(kernel, (nx, ny, nz, layers, rows, cols, steps, listed)),
             out_shape=[jax.ShapeDtypeStruct(flat, f32)] * 2,
-            in_specs=[hbm] * 7 + [pl.BlockSpec(memory_space=pltpu.SMEM)],
+            in_specs=[hbm] * 8,
             out_specs=[vmem, vmem],
             scratch_shapes=[
                 pltpu.VMEM((6, cells, cols), f32),
                 pltpu.VMEM((steps, listed), f32),
                 pltpu.VMEM((1, listed), jnp.int32),
                 pltpu.VMEM((1, listed), jnp.int32),
+                pltpu.SMEM(substeps.shape, jnp.int32),
                 pltpu.VMEM((height, cols), f32),
                 pltpu.VMEM((tiles, height, cols), f32),
                 pltpu.VMEM((2, wide, cols), f32),
@@ -574,14 +586,15 @@
                 pltpu.VMEM((turns, 2, SUB, cols), f32),
                 pltpu.VMEM((turns, 2, SUB, cols), f32),
                 pltpu.VMEM((turns, 2, rows, cols), f32),
-                pltpu.SemaphoreType.DMA((7,)),
+                pltpu.VMEM((steps, cells, cols), f32),
+                pltpu.SemaphoreType.DMA((8,)),
                 pltpu.SemaphoreType.DMA((tiles,)),
                 pltpu.SemaphoreType.DMA((tiles,)),
                 pltpu.SemaphoreType.DMA((steps, 6)),
                 pltpu.SemaphoreType.DMA((steps, 6)),
             ],
             compiler_params=pltpu.CompilerParams(
-                collective_id=0, has_side_effects=True, vmem_limit_bytes=32 * 1024 * 1024
+                collective_id=0, has_side_effects=True, vmem_limit_bytes=63 * 1024 * 1024
             ),
         )(
             conductivity.reshape(3, *flat),

time: 26.2 us -> 23.4 us (0.89)
  local copies, waits for them, and re-layouts: 5.08 us -> 2 us
  Pallas kernels: 20.1 us -> 20.5 us
    unnamed x18 -> x4, local copies, waits for them, and re-layouts: 5.08 us -> 2 us
    pallas_call x1, Pallas kernels: 20.1 us -> 20.5 us  [body(): pl.pallas_call(functools.partial(kernel, (nx, ny, nz, layers, rows, cols,...]
where the time goes in v2:
time: 23.4 us; the launch traced here: 23.2 us
  Pallas kernels  20.5 us (88%)
  local copies, waits for them, and re-layouts  2 us (9%)
  between operations  0.65 us (3%)
    pallas_call x1, Pallas kernels, body(): pl.pallas_call(functools.partial(kernel, (nx, ny, nz, layers, rows, cols,...  20.5 us
    unnamed x4, local copies, waits for them, and re-layouts  2 us

profile of v2, /device:TPU:0, one launch (start us, length us, event | category | flops | bytes accessed | tf_op | source)
XLA Modules:
  0.0 23.2 jit_solution(11867765789097055035)
XLA Ops:
  0.6 20.5 %shard_map.95 = (f32[64,128]{1,0:T(8,128)}, f32[64,128]{1,0:T(8,128)}) custom-call(f32[3,64,128]{2,1,0:T(8,128)} %bitcast.8, f32[64,128]{1,0:T(8,128)} %bitcast.9, f32[64,128]{1,0:T(8,128)} %bitcast.10, f32[64,128]{1,0:T(8,128)} %bitcast.11, f32[4,64]{1,0:T(4,128)} %res_hbm.1, s32[1,64]{1,0:T(1,128)} %bitcast.14, s32[1,64]{1,0:T(1,128)} %bitcast.15, ...), custom_call_target="tpu_custom_call" | custom-call | tf_op jit(solution)/shard_map/pallas_call | solution.py:565
  21.2 0.0 copy-start
  21.2 1.4 %copy.12 = f32[4,16,128]{2,1,0:T(8,128)} copy(f32[4,16,128]{2,1,0:T(8,128)} %bitcast.13) | data formatting | bytes 65536
  22.6 0.0 copy-done
  22.6 0.6 %copy.13 = f32[4,16,128]{2,1,0:T(8,128)} copy(f32[4,16,128]{2,1,0:T(8,128)S(1)} %bitcast.12) | data formatting | bytes 65536
Async XLA Ops:
  21.2 1.4 %copy-start = (f32[64,128]{1,0:T(8,128)S(1)}, f32[64,128]{1,0:T(8,128)}, u32[]{:S(2)}) copy-start(f32[64,128]{1,0:T(8,128)} %get-tuple-element.5) | copy-start | bytes 98308

commit v3 on v1

--- a/solution.py
+++ b/solution.py
@@ -34,7 +34,8 @@
     tile_hbm,
     cell_hbm,
     substeps_hbm,
-    adjoint_out,
+    kept_out,
+    moved_out,
     sens_out,
     base,
     res_in,
@@ -141,6 +142,37 @@
         sensors[...] = jnp.where(mine, sensors[...], 0.0)
     gathered[me] = sensors[...]
 
+    neighbours = (
+        (tiles - 1)
+        + (z > 0).astype(jnp.int32)
+        + (z < nz - 1).astype(jnp.int32)
+    )
+    pl.semaphore_wait(barrier, neighbours)
+
+    def sensor_copy(offset):
+        return pltpu.make_async_remote_copy(
+            src_ref=sensors,
+            dst_ref=gathered.at[me],
+            send_sem=sensor_send.at[offset],
+            recv_sem=sensor_recv.at[offset],
+            device_id=sensor_peer(offset),
+            device_id_type=MESH,
+        )
+
+    def sensor_arrival(offset):
+        origin = lax.rem(me + (tiles - offset), tiles)
+        return pltpu.make_async_remote_copy(
+            src_ref=sensors,
+            dst_ref=gathered.at[origin],
+            send_sem=sensor_send.at[offset],
+            recv_sem=sensor_recv.at[offset],
+            device_id=sensor_peer(offset),
+            device_id_type=MESH,
+        )
+
+    for offset in range(1, tiles):
+        sensor_copy(offset).start()
+
     for load in loads[3:]:
         load.wait()
     lanes = lax.broadcasted_iota(jnp.int32, (SUB, cols), 1)
@@ -184,41 +216,6 @@
 
     c0, c1, c2 = base[0], base[1], base[2]
     adjoint, ratio, rate = base[3], base[4], base[5]
-
-    for k, array in enumerate((adjoint, ratio, c0)):
-        first_x[0, k * layers : (k + 1) * layers, :] = pick_rows(array, 0)
-        first_x[1, k * layers : (k + 1) * layers, :] = pick_rows(array, rows - 1)
-    left, right = pack_columns((adjoint, ratio, c1))
-    first_y[0] = left
-    first_y[1] = right
-
-    neighbours = (
-        (tiles - 1)
-        + (z > 0).astype(jnp.int32)
-        + (z < nz - 1).astype(jnp.int32)
-    )
-    pl.semaphore_wait(barrier, neighbours)
-
-    def sensor_copy(offset):
-        return pltpu.make_async_remote_copy(
-            src_ref=sensors,
-            dst_ref=gathered.at[me],
-            send_sem=sensor_send.at[offset],
-            recv_sem=sensor_recv.at[offset],
-            device_id=sensor_peer(offset),
-            device_id_type=MESH,
-        )
-
-    def sensor_arrival(offset):
-        origin = lax.rem(me + (tiles - offset), tiles)
-        return pltpu.make_async_remote_copy(
-            src_ref=sensors,
-            dst_ref=gathered.at[origin],
-            send_sem=sensor_send.at[offset],
-            recv_sem=sensor_recv.at[offset],
-            device_id=sensor_peer(offset),
-            device_id_type=MESH,
-        )
 
     def halo_copies(turn):
         copies = []
@@ -280,9 +277,15 @@
             pl.when(valid)(copy.wait_send)
 
     copies = halo_copies(0)
-    for offset in range(1, tiles):
-        sensor_copy(offset).start()
-    start(copies, (2, 3, 4, 5, 0, 1))
+    start(copies, (4, 5))
+    for k, array in enumerate((adjoint, ratio, c0)):
+        first_x[0, k * layers : (k + 1) * layers, :] = pick_rows(array, 0)
+        first_x[1, k * layers : (k + 1) * layers, :] = pick_rows(array, rows - 1)
+    left, right = pack_columns((adjoint, ratio, c1))
+    first_y[0] = left
+    first_y[1] = right
+
+    start(copies, (2, 3, 0, 1))
 
     full = (cells, cols)
     row_in = lax.rem(lax.broadcasted_iota(jnp.int32, full, 0), rows)
@@ -330,14 +333,16 @@
         + jnp.concatenate([no_layer, between], axis=0)
     )
 
-    def refine(field):
-        for turn in range(MOST_TURNS):
-            after = (
-                stay * field
-                + (rate_next_row * next_row(field) + rate_prev_row * prev_row(field))
-                + (rate_next_col * next_col(field) + rate_prev_col * prev_col(field))
-            )
-            field = jnp.where(turns > turn, after, field)
+    def halves(field):
+        around_it = (rate_next_row * next_row(field) + rate_prev_row * prev_row(field)) + (
+            rate_next_col * next_col(field) + rate_prev_col * prev_col(field)
+        )
+        return stay * field, around_it
+
+    def refine(field, count):
+        for turn in range(count):
+            kept, moved = halves(field)
+            field = jnp.where(turns > turn, kept + moved, field)
         return field
 
     def inner(field, weighted, own):
@@ -355,37 +360,8 @@
         place = lax.broadcasted_iota(jnp.int32, (count, cols), 0).astype(jnp.float32)
         return place + (row_key + start_at)
 
-    arrive(copies)
     for offset in range(1, tiles):
         sensor_arrival(offset).wait_recv()
-
-    row_halo = spread_rows(
-        first_x_in[0, 2 * layers : 3 * layers, :], first_x_in[1, 2 * layers : 3 * layers, :]
-    )
-    row_face = jnp.where(jnp.logical_or(top, bottom), harmonic(c0, row_halo), 0.0)
-    packed = first_y_in[0] + first_y_in[1]
-    col_halo = unpack_columns(packed, 2 * groups_of_rows)
-    col_face = jnp.where(jnp.logical_or(first_col, last_col), harmonic(c1, col_halo), 0.0)
-    low_face = harmonic(c2[:rows], first_z_in[0, 0])
-    high_face = harmonic(c2[cells - rows :], first_z_in[1, 0])
-    middle = cells - 2 * rows
-
-    def with_ends(low, high):
-        parts = [low]
-        if middle > 0:
-            parts.append(jnp.zeros((middle, cols), jnp.float32))
-        return jnp.concatenate(parts + [high], axis=0)
-
-    all_faces = inner_faces + row_face + col_face + with_ends(low_face, high_face)
-    own = 1.0 - ratio * all_faces
-
-    def outer(row_values, col_values, low_values, high_values):
-        return (
-            row_face * row_values
-            + col_face * col_values
-            + with_ends(low_face * low_values, high_face * high_values)
-        )
-
     blocks = []
     folded = max(1, tiles // per)
     for block in range(folded):
@@ -455,20 +431,41 @@
     ]
     at_edges = jnp.concatenate(
         [
-            jnp.where(
-                jnp.logical_or(
-                    jnp.logical_and(col_ids == 0.0, line == cols - 1.0),
-                    jnp.logical_and(col_ids == cols - 1.0, line == 0.0),
-                ),
-                1.0,
-                0.0,
-            ).astype(jnp.bfloat16)
+            jnp.where(col_ids == (cols - 1.0) - line, 1.0, 0.0).astype(jnp.bfloat16)
             for line in col_rows
         ],
         axis=1,
     )
     edge = source_of(own_keys, moved_keys, at_edges, last)
-    next_source = source_of(own_keys, key_rows, in_column, last - 1)
+
+    arrive(copies)
+
+    row_halo = spread_rows(
+        first_x_in[0, 2 * layers : 3 * layers, :], first_x_in[1, 2 * layers : 3 * layers, :]
+    )
+    row_face = jnp.where(jnp.logical_or(top, bottom), harmonic(c0, row_halo), 0.0)
+    packed = first_y_in[0] + first_y_in[1]
+    col_halo = unpack_columns(packed, 2 * groups_of_rows)
+    col_face = jnp.where(jnp.logical_or(first_col, last_col), harmonic(c1, col_halo), 0.0)
+    low_face = harmonic(c2[:rows], first_z_in[0, 0])
+    high_face = harmonic(c2[cells - rows :], first_z_in[1, 0])
+    middle = cells - 2 * rows
+
+    def with_ends(low, high):
+        parts = [low]
+        if middle > 0:
+            parts.append(jnp.zeros((middle, cols), jnp.float32))
+        return jnp.concatenate(parts + [high], axis=0)
+
+    all_faces = inner_faces + row_face + col_face + with_ends(low_face, high_face)
+    own = 1.0 - ratio * all_faces
+
+    def outer(row_values, col_values, low_values, high_values):
+        return (
+            row_face * row_values
+            + col_face * col_values
+            + with_ends(low_face * low_values, high_face * high_values)
+        )
 
     field = adjoint + wide[:cells]
     low_src = wide[cells : cells + rows]
@@ -488,7 +485,8 @@
         first_z_in[0, 2] * (first_z_in[0, 1] + low_src),
         first_z_in[1, 2] * (first_z_in[1, 1] + high_src),
     )
-    field = refine(field)
+    next_source = source_of(own_keys, key_rows, in_column, last - 1)
+    field = refine(field, MOST_TURNS)
     sens = ratio * field
 
     pending = [copies]
@@ -519,14 +517,19 @@
             recv_z[at, 0],
             recv_z[at, 1],
         )
-        field = refine(field)
-        sens = sens + ratio * field
-
-    results[0] = field
-    results[1] = sens
+        if step > 0:
+            field = refine(field, MOST_TURNS)
+            sens = sens + ratio * field
+
+    field = refine(field, MOST_TURNS - 1)
+    kept, moved = halves(field)
+    active = turns > MOST_TURNS - 1
+    results[0] = jnp.where(active, kept, field)
+    results[1] = jnp.where(active, moved, 0.0)
+    results[2] = sens
     stores = [
         pltpu.make_async_copy(results.at[k], out, store_sem.at[k])
-        for k, out in enumerate((adjoint_out, sens_out))
+        for k, out in enumerate((kept_out, moved_out, sens_out))
     ]
     for store in stores:
         store.start()
@@ -536,17 +539,6 @@
         sent(copies)
     for store in stores:
         store.wait()
-
-
-def deliver(first, second, first_out, second_out, sems):
-    copies = (
-        pltpu.make_async_copy(first, first_out, sems.at[0]),
-        pltpu.make_async_copy(second, second_out, sems.at[1]),
-    )
-    for copy in copies:
-        copy.start()
-    for copy in copies:
-        copy.wait()
 
 
 def solution(mesh):
@@ -573,11 +565,11 @@
         turns = steps - 1
         f32 = jnp.float32
         hbm = pl.BlockSpec(memory_space=pltpu.HBM)
-        adjoint, sens = pl.pallas_call(
+        kept, moved, sens = pl.pallas_call(
             functools.partial(kernel, (nx, ny, nz, layers, rows, cols, steps, listed)),
-            out_shape=[jax.ShapeDtypeStruct(flat, f32)] * 2,
+            out_shape=[jax.ShapeDtypeStruct(flat, f32)] * 3,
             in_specs=[hbm] * 8,
-            out_specs=[hbm, hbm],
+            out_specs=[hbm] * 3,
             scratch_shapes=[
                 pltpu.VMEM((6, cells, cols), f32),
                 pltpu.VMEM((steps, listed), f32),
@@ -597,9 +589,9 @@
                 pltpu.VMEM((turns, 2, SUB, cols), f32),
                 pltpu.VMEM((turns, 2, SUB, cols), f32),
                 pltpu.VMEM((turns, 2, rows, cols), f32),
-                pltpu.VMEM((2, cells, cols), f32),
+                pltpu.VMEM((3, cells, cols), f32),
                 pltpu.SemaphoreType.DMA((8,)),
-                pltpu.SemaphoreType.DMA((2,)),
+                pltpu.SemaphoreType.DMA((3,)),
                 pltpu.SemaphoreType.DMA((tiles,)),
                 pltpu.SemaphoreType.DMA((tiles,)),
                 pltpu.SemaphoreType.DMA((steps, 6)),
@@ -618,15 +610,9 @@
             sensor_cell.reshape(1, listed),
             substeps,
         )
-        adjoint, sens = pl.pallas_call(
-            deliver,
-            out_shape=[jax.ShapeDtypeStruct(flat, f32)] * 2,
-            in_specs=[hbm, hbm],
-            out_specs=[hbm, hbm],
-            scratch_shapes=[pltpu.SemaphoreType.DMA((2,))],
-            compiler_params=pltpu.CompilerParams(vmem_limit_bytes=63 * 1024 * 1024),
-        )(adjoint, sens)
-        return adjoint.reshape(layers, rows, cols), sens.reshape(layers, rows, cols)
+        shape = adjoint_final.shape
+        adjoint = kept.reshape(shape) + moved.reshape(shape)
+        return adjoint, sens.reshape(shape) + step_ratio * adjoint
 
     return jax.shard_map(
         body,

time: 24.1 us -> 22.2 us (0.921)
  Pallas kernels: 23.3 us -> 19.9 us
  other arithmetic: 0 us -> 1.41 us
    pallas_call x1 -> x0, Pallas kernels: 3.11 us -> none  [body(): pl.pallas_call(deliver, out_shape=[jax.ShapeDtypeStruct(flat, f32)] * 2,...]
    add x0 -> x2, other arithmetic: none -> 1.41 us  [the longest x1 0.79 us: body(): adjoint = kept.reshape(shape) + moved.reshape(shape)]
    pallas_call x1, Pallas kernels: 20.2 us -> 19.9 us  [body(): pl.pallas_call(functools.partial(kernel, (nx, ny, nz, layers, rows, cols,...]
where the time goes in v3:
time: 22.2 us; the launch traced here: 22 us
  Pallas kernels  19.9 us (90%)
  other arithmetic  1.41 us (6%)
  between operations  0.67 us (3%)
    pallas_call x1, Pallas kernels, body(): pl.pallas_call(functools.partial(kernel, (nx, ny, nz, layers, rows, cols,...  19.9 us
    add x1, other arithmetic, body(): adjoint = kept.reshape(shape) + moved.reshape(shape)  0.79 us
    add x1, other arithmetic, body(): return (adjoint, sens.reshape(shape) + step_ratio * adjoint)  0.62 us

profile of v3, /device:TPU:0, one launch (start us, length us, event | category | flops | bytes accessed | tf_op | source)
XLA Modules:
  0.0 22.0 jit_solution(6641068140468097739)
XLA Ops:
  0.6 19.9 %shard_map.95 = (f32[64,128]{1,0:T(8,128)}, f32[64,128]{1,0:T(8,128)}, f32[64,128]{1,0:T(8,128)}) custom-call(f32[3,64,128]{2,1,0:T(8,128)} %bitcast.11, f32[64,128]{1,0:T(8,128)} %bitcast.12, f32[64,128]{1,0:T(8,128)} %bitcast.8, f32[64,128]{1,0:T(8,128)} %bitcast.13, f32[4,64]{1,0:T(4,128)} %res_hbm.1, s32[1,64]{1,0:T(1,128)} %bitcast.15, ...), custom_call_target="tpu_custom_call" | custom-call | tf_op jit(solution)/shard_map/pallas_call | solution.py:568
  20.5 0.0 copy-start
  20.5 0.0 copy-start.2
  20.5 0.8 %add.9 = f32[64,128]{1,0:T(8,128)S(1)} add(f32[64,128]{1,0:T(8,128)} %get-tuple-element.5, f32[64,128]{1,0:T(8,128)} %get-tuple-element.6) | non-fusion elementwise | flops 8192 | bytes 98304 | tf_op jit(solution)/shard_map/add | solution.py:614
  21.3 0.0 copy-start.1
  21.3 0.0 copy-done
  21.3 0.0 copy-done.2
  21.3 0.6 %multiply_add_fusion = f32[4,16,128]{2,1,0:T(8,128)} fusion(f32[4,16,128]{2,1,0:T(8,128)S(1)} %bitcast.14, f32[4,16,128]{2,1,0:T(8,128)S(1)} %copy-done, f32[4,16,128]{2,1,0:T(8,128)S(1)} %bitcast.9), kind=kLoop, calls=%fused_computation | loop fusion | flops 16384 | bytes 131072 | tf_op jit(solution)/shard_map/add | solution.py:615
  22.0 0.0 copy-done.1
Async XLA Ops:
  20.5 0.8 %copy-start = (f32[4,16,128]{2,1,0:T(8,128)S(1)}, f32[4,16,128]{2,1,0:T(8,128)}, u32[]{:S(2)}) copy-start(f32[4,16,128]{2,1,0:T(8,128)} %param.10) | copy-start | bytes 98308
  20.5 0.8 %copy-start.2 = (f32[64,128]{1,0:T(8,128)S(1)}, f32[64,128]{1,0:T(8,128)}, u32[]{:S(2)}) copy-start(f32[64,128]{1,0:T(8,128)} %get-tuple-element.7) | copy-start | bytes 98308
  21.3 0.6 %copy-start.1 = (f32[64,128]{1,0:T(8,128)}, f32[64,128]{1,0:T(8,128)S(1)}, u32[]{:S(2)}) copy-start(f32[64,128]{1,0:T(8,128)S(1)} %add.9) | copy-start | bytes 98308

commit v4 on v3

--- a/solution.py
+++ b/solution.py
@@ -56,6 +56,7 @@
     recv_y,
     recv_z,
     results,
+    shifted,
     load_sem,
     store_sem,
     sensor_send,
@@ -88,7 +89,7 @@
     for load in loads:
         load.start()
 
-    for ref in (first_x_in, first_y_in, first_z_in, recv_x, recv_y, recv_z, sensors):
+    for ref in (first_x_in, first_y_in, first_z_in, recv_x, recv_y, recv_z, sensors, shifted):
         ref[...] = jnp.zeros_like(ref)
 
     sides = (
@@ -268,8 +269,9 @@
             valid, copy, _ = copies[side]
             pl.when(valid)(copy.start)
 
-    def arrive(copies):
-        for valid, _, arrival in copies:
+    def arrive(copies, chosen):
+        for side in chosen:
+            valid, _, arrival = copies[side]
             pl.when(valid)(arrival.wait_recv)
 
     def sent(copies):
@@ -333,15 +335,19 @@
         + jnp.concatenate([no_layer, between], axis=0)
     )
 
-    def halves(field):
-        around_it = (rate_next_row * next_row(field) + rate_prev_row * prev_row(field)) + (
+    def halves(field, turn):
+        half = turn % 2
+        shifted[half, SUB : SUB + cells, :] = field
+        below = shifted[half, SUB + 1 : SUB + 1 + cells, :]
+        above = shifted[half, SUB - 1 : SUB - 1 + cells, :]
+        around_it = (rate_next_row * below + rate_prev_row * above) + (
             rate_next_col * next_col(field) + rate_prev_col * prev_col(field)
         )
         return stay * field, around_it
 
     def refine(field, count):
         for turn in range(count):
-            kept, moved = halves(field)
+            kept, moved = halves(field, turn)
             field = jnp.where(turns > turn, kept + moved, field)
         return field
 
@@ -438,15 +444,11 @@
     )
     edge = source_of(own_keys, moved_keys, at_edges, last)
 
-    arrive(copies)
-
+    arrive(copies, (0, 1, 4, 5))
     row_halo = spread_rows(
         first_x_in[0, 2 * layers : 3 * layers, :], first_x_in[1, 2 * layers : 3 * layers, :]
     )
     row_face = jnp.where(jnp.logical_or(top, bottom), harmonic(c0, row_halo), 0.0)
-    packed = first_y_in[0] + first_y_in[1]
-    col_halo = unpack_columns(packed, 2 * groups_of_rows)
-    col_face = jnp.where(jnp.logical_or(first_col, last_col), harmonic(c1, col_halo), 0.0)
     low_face = harmonic(c2[:rows], first_z_in[0, 0])
     high_face = harmonic(c2[cells - rows :], first_z_in[1, 0])
     middle = cells - 2 * rows
@@ -457,38 +459,46 @@
             parts.append(jnp.zeros((middle, cols), jnp.float32))
         return jnp.concatenate(parts + [high], axis=0)
 
-    all_faces = inner_faces + row_face + col_face + with_ends(low_face, high_face)
-    own = 1.0 - ratio * all_faces
-
-    def outer(row_values, col_values, low_values, high_values):
-        return (
-            row_face * row_values
-            + col_face * col_values
-            + with_ends(low_face * low_values, high_face * high_values)
-        )
+    near_faces = inner_faces + row_face + with_ends(low_face, high_face)
+    row_values = spread_rows(
+        first_x_in[0, layers : 2 * layers, :]
+        * (first_x_in[0, 0:layers, :] + wide[cells + 2 * rows : cells + 2 * rows + layers]),
+        first_x_in[1, layers : 2 * layers, :]
+        * (
+            first_x_in[1, 0:layers, :]
+            + wide[cells + 2 * rows + layers : cells + 2 * rows + 2 * layers]
+        ),
+    )
+    low_values = first_z_in[0, 2] * (first_z_in[0, 1] + wide[cells : cells + rows])
+    high_values = first_z_in[1, 2] * (first_z_in[1, 1] + wide[cells + rows : cells + 2 * rows])
+
+    def outer(row_values, low_values, high_values):
+        return row_face * row_values + with_ends(
+            low_face * low_values, high_face * high_values
+        )
+
+    arrive(copies, (2, 3))
+    packed = first_y_in[0] + first_y_in[1]
+    col_halo = unpack_columns(packed, 2 * groups_of_rows)
+    col_face = jnp.where(jnp.logical_or(first_col, last_col), harmonic(c1, col_halo), 0.0)
+    own = 1.0 - ratio * (near_faces + col_face)
 
     field = adjoint + wide[:cells]
-    low_src = wide[cells : cells + rows]
-    high_src = wide[cells + rows : cells + 2 * rows]
-    side_src = wide[cells + 2 * rows : cells + 2 * rows + 2 * layers]
-    rows_low = first_x_in[0, layers : 2 * layers, :] * (
-        first_x_in[0, 0:layers, :] + side_src[:layers]
-    )
-    rows_high = first_x_in[1, layers : 2 * layers, :] * (
-        first_x_in[1, 0:layers, :] + side_src[layers:]
-    )
     cols_adjoint = unpack_columns(packed, 0)
     cols_ratio = unpack_columns(packed, groups_of_rows)
-    field = inner(field, ratio * field, own) + outer(
-        spread_rows(rows_low, rows_high),
-        cols_ratio * (cols_adjoint + edge),
-        first_z_in[0, 2] * (first_z_in[0, 1] + low_src),
-        first_z_in[1, 2] * (first_z_in[1, 1] + high_src),
+    field = (
+        inner(field, ratio * field, own)
+        + outer(row_values, low_values, high_values)
+        + col_face * (cols_ratio * (cols_adjoint + edge))
     )
     next_source = source_of(own_keys, key_rows, in_column, last - 1)
     field = refine(field, MOST_TURNS)
     sens = ratio * field
 
+    stores = [
+        pltpu.make_async_copy(results.at[k], out, store_sem.at[k])
+        for k, out in enumerate((kept_out, moved_out, sens_out))
+    ]
     pending = [copies]
     sources = {last - 1: next_source}
     for turn in range(1, steps):
@@ -507,31 +517,30 @@
         send_x[at, 1, 0:layers, :] = pick_rows(weighted, rows - 1)
         start(copies, (0, 1))
         pending.append(copies)
+        if step == 0:
+            results[2] = sens
+            stores[2].start()
         field = inner(field, weighted, own)
         if step > 0:
             sources[step - 1] = source_of(own_keys, key_rows, in_column, step - 1)
-        arrive(copies)
+        arrive(copies, (0, 1, 4, 5))
         field = field + outer(
             spread_rows(recv_x[at, 0, 0:layers, :], recv_x[at, 1, 0:layers, :]),
-            unpack_columns(recv_y[at, 0] + recv_y[at, 1], 0),
             recv_z[at, 0],
             recv_z[at, 1],
         )
+        arrive(copies, (2, 3))
+        field = field + col_face * unpack_columns(recv_y[at, 0] + recv_y[at, 1], 0)
         if step > 0:
             field = refine(field, MOST_TURNS)
             sens = sens + ratio * field
 
     field = refine(field, MOST_TURNS - 1)
-    kept, moved = halves(field)
+    kept, moved = halves(field, MOST_TURNS - 1)
     active = turns > MOST_TURNS - 1
     results[0] = jnp.where(active, kept, field)
     results[1] = jnp.where(active, moved, 0.0)
-    results[2] = sens
-    stores = [
-        pltpu.make_async_copy(results.at[k], out, store_sem.at[k])
-        for k, out in enumerate((kept_out, moved_out, sens_out))
-    ]
-    for store in stores:
+    for store in stores[:2]:
         store.start()
     for offset in range(1, tiles):
         sensor_copy(offset).wait_send()
@@ -590,6 +599,7 @@
                 pltpu.VMEM((turns, 2, SUB, cols), f32),
                 pltpu.VMEM((turns, 2, rows, cols), f32),
                 pltpu.VMEM((3, cells, cols), f32),
+                pltpu.VMEM((2, cells + 2 * SUB, cols), f32),
                 pltpu.SemaphoreType.DMA((8,)),
                 pltpu.SemaphoreType.DMA((3,)),
                 pltpu.SemaphoreType.DMA((tiles,)),

time: 22.2 us -> 22.3 us (level)
  no operation moved by 1% of the time
where the time goes in v4:
time: 22.3 us; the launch traced here: 22.1 us
  Pallas kernels  20 us (90%)
  other arithmetic  1.41 us (6%)
  between operations  0.67 us (3%)
    pallas_call x1, Pallas kernels, body(): pl.pallas_call(functools.partial(kernel, (nx, ny, nz, layers, rows, cols,...  20 us
    add x1, other arithmetic, body(): adjoint = kept.reshape(shape) + moved.reshape(shape)  0.79 us
    add x1, other arithmetic, body(): return (adjoint, sens.reshape(shape) + step_ratio * adjoint)  0.62 us

profile of v4, /device:TPU:0, one launch (start us, length us, event | category | flops | bytes accessed | tf_op | source)
XLA Modules:
  0.0 22.1 jit_solution(18069201637791619705)
XLA Ops:
  0.6 20.0 %shard_map.95 = (f32[64,128]{1,0:T(8,128)}, f32[64,128]{1,0:T(8,128)}, f32[64,128]{1,0:T(8,128)}) custom-call(f32[3,64,128]{2,1,0:T(8,128)} %bitcast.11, f32[64,128]{1,0:T(8,128)} %bitcast.12, f32[64,128]{1,0:T(8,128)} %bitcast.8, f32[64,128]{1,0:T(8,128)} %bitcast.13, f32[4,64]{1,0:T(4,128)} %res_hbm.1, s32[1,64]{1,0:T(1,128)} %bitcast.15, ...), custom_call_target="tpu_custom_call" | custom-call | tf_op jit(solution)/shard_map/pallas_call | solution.py:577
  20.6 0.0 copy-start
  20.6 0.0 copy-start.2
  20.6 0.8 %add.9 = f32[64,128]{1,0:T(8,128)S(1)} add(f32[64,128]{1,0:T(8,128)} %get-tuple-element.5, f32[64,128]{1,0:T(8,128)} %get-tuple-element.6) | non-fusion elementwise | flops 8192 | bytes 98304 | tf_op jit(solution)/shard_map/add | solution.py:624
  21.4 0.0 copy-start.1
  21.4 0.0 copy-done
  21.4 0.0 copy-done.2
  21.4 0.6 %multiply_add_fusion = f32[4,16,128]{2,1,0:T(8,128)} fusion(f32[4,16,128]{2,1,0:T(8,128)S(1)} %bitcast.14, f32[4,16,128]{2,1,0:T(8,128)S(1)} %copy-done, f32[4,16,128]{2,1,0:T(8,128)S(1)} %bitcast.9), kind=kLoop, calls=%fused_computation | loop fusion | flops 16384 | bytes 131072 | tf_op jit(solution)/shard_map/add | solution.py:625
  22.1 0.0 copy-done.1
Async XLA Ops:
  20.6 0.8 %copy-start = (f32[4,16,128]{2,1,0:T(8,128)S(1)}, f32[4,16,128]{2,1,0:T(8,128)}, u32[]{:S(2)}) copy-start(f32[4,16,128]{2,1,0:T(8,128)} %param.10) | copy-start | bytes 98308
  20.6 0.8 %copy-start.2 = (f32[64,128]{1,0:T(8,128)S(1)}, f32[64,128]{1,0:T(8,128)}, u32[]{:S(2)}) copy-start(f32[64,128]{1,0:T(8,128)} %get-tuple-element.7) | copy-start | bytes 98308
  21.4 0.6 %copy-start.1 = (f32[64,128]{1,0:T(8,128)}, f32[64,128]{1,0:T(8,128)S(1)}, u32[]{:S(2)}) copy-start(f32[64,128]{1,0:T(8,128)S(1)} %add.9) | copy-start | bytes 98308

commit v5 on v4

--- a/solution.py
+++ b/solution.py
@@ -507,12 +507,12 @@
         weighted = ratio * field
         copies = halo_copies(turn)
         at = turn - 1
-        send_w[at] = weighted
-        start(copies, (4, 5))
         left, right = pack_columns((weighted,))
         send_y[at, 0] = left
         send_y[at, 1] = right
         start(copies, (2, 3))
+        send_w[at] = weighted
+        start(copies, (4, 5))
         send_x[at, 0, 0:layers, :] = pick_rows(weighted, 0)
         send_x[at, 1, 0:layers, :] = pick_rows(weighted, rows - 1)
         start(copies, (0, 1))
@@ -621,8 +621,9 @@
             substeps,
         )
         shape = adjoint_final.shape
-        adjoint = kept.reshape(shape) + moved.reshape(shape)
-        return adjoint, sens.reshape(shape) + step_ratio * adjoint
+        adjoint = kept + moved
+        sensitivity = sens + step_ratio.reshape(flat) * adjoint
+        return adjoint.reshape(shape), sensitivity.reshape(shape)
 
     return jax.shard_map(
         body,

time: 22.3 us -> 22.5 us (level)
    pallas_call x1, Pallas kernels: 20 us -> 20.2 us  [body(): pl.pallas_call(functools.partial(kernel, (nx, ny, nz, layers, rows, cols,...]
    add x2 -> x1, other arithmetic: 1.41 us -> 1.42 us  [body(): sensitivity = sens + step_ratio.reshape(flat) * adjoint]
where the time goes in v5:
time: 22.5 us; the launch traced here: 22.3 us
  Pallas kernels  20.2 us (90%)
  other arithmetic  1.42 us (6%)
  between operations  0.66 us (3%)
    pallas_call x1, Pallas kernels, body(): pl.pallas_call(functools.partial(kernel, (nx, ny, nz, layers, rows, cols,...  20.2 us
    add x1, other arithmetic, body(): sensitivity = sens + step_ratio.reshape(flat) * adjoint  1.42 us

profile of v5, /device:TPU:0, one launch (start us, length us, event | category | flops | bytes accessed | tf_op | source)
XLA Modules:
  0.0 22.3 jit_solution(6353733868780770097)
XLA Ops:
  0.6 0.0 copy-start
  0.6 20.2 %shard_map.95 = (f32[64,128]{1,0:T(8,128)}, f32[64,128]{1,0:T(8,128)}, f32[64,128]{1,0:T(8,128)}) custom-call(f32[3,64,128]{2,1,0:T(8,128)} %bitcast.10, f32[64,128]{1,0:T(8,128)} %bitcast.11, f32[64,128]{1,0:T(8,128)} %bitcast.9, f32[64,128]{1,0:T(8,128)} %bitcast.12, f32[4,64]{1,0:T(4,128)} %res_hbm.1, s32[1,64]{1,0:T(1,128)} %bitcast.15, ...), custom_call_target="tpu_custom_call" | custom-call | tf_op jit(solution)/shard_map/pallas_call | solution.py:577
  20.9 0.0 copy-done
  20.9 1.4 %multiply_add_fusion = (f32[64,128]{1,0:T(8,128)}, f32[64,128]{1,0:T(8,128)}) fusion(f32[64,128]{1,0:T(8,128)} %get-tuple-element.7, f32[4,16,128]{2,1,0:T(8,128)S(1)} %copy-done, f32[64,128]{1,0:T(8,128)} %get-tuple-element.5, f32[64,128]{1,0:T(8,128)} %get-tuple-element.6), kind=kLoop, calls=%fused_computation | loop fusion | flops 24576 | bytes 196608 | tf_op jit(solution)/shard_map/add | solution.py:625
Async XLA Ops:
  0.6 20.2 %copy-start = (f32[4,16,128]{2,1,0:T(8,128)S(1)}, f32[4,16,128]{2,1,0:T(8,128)}, u32[]{:S(2)}) copy-start(f32[4,16,128]{2,1,0:T(8,128)} %param.10) | copy-start | bytes 98308

commit v6 on v3

--- a/solution.py
+++ b/solution.py
@@ -85,9 +85,6 @@
             )
         )
     ]
-    for load in loads:
-        load.start()
-
     for ref in (first_x_in, first_y_in, first_z_in, recv_x, recv_y, recv_z, sensors):
         ref[...] = jnp.zeros_like(ref)
 
@@ -123,6 +120,9 @@
             pl.semaphore_signal(
                 barrier, inc=1, device_id=device_at(axis, step), device_id_type=MESH
             )
+
+    for load in loads:
+        load.start()
 
     for load in loads[:3]:
         load.wait()
@@ -278,14 +278,15 @@
 
     copies = halo_copies(0)
     start(copies, (4, 5))
+    left, right = pack_columns((adjoint, ratio, c1))
+    first_y[0] = left
+    first_y[1] = right
+
+    start(copies, (2, 3))
     for k, array in enumerate((adjoint, ratio, c0)):
         first_x[0, k * layers : (k + 1) * layers, :] = pick_rows(array, 0)
         first_x[1, k * layers : (k + 1) * layers, :] = pick_rows(array, rows - 1)
-    left, right = pack_columns((adjoint, ratio, c1))
-    first_y[0] = left
-    first_y[1] = right
-
-    start(copies, (2, 3, 0, 1))
+    start(copies, (0, 1))
 
     full = (cells, cols)
     row_in = lax.rem(lax.broadcasted_iota(jnp.int32, full, 0), rows)

time: 22.2 us -> 22.3 us (level)
  no operation moved by 1% of the time
where the time goes in v6:
time: 22.3 us; the launch traced here: 22.1 us
  Pallas kernels  20 us (90%)
  other arithmetic  1.41 us (6%)
  between operations  0.67 us (3%)
    pallas_call x1, Pallas kernels, body(): pl.pallas_call(functools.partial(kernel, (nx, ny, nz, layers, rows, cols,...  20 us
    add x1, other arithmetic, body(): adjoint = kept.reshape(shape) + moved.reshape(shape)  0.79 us
    add x1, other arithmetic, body(): return (adjoint, sens.reshape(shape) + step_ratio * adjoint)  0.62 us

profile of v6, /device:TPU:0, one launch (start us, length us, event | category | flops | bytes accessed | tf_op | source)
XLA Modules:
  0.0 22.1 jit_solution(10999077882667679649)
XLA Ops:
  0.6 20.0 %shard_map.95 = (f32[64,128]{1,0:T(8,128)}, f32[64,128]{1,0:T(8,128)}, f32[64,128]{1,0:T(8,128)}) custom-call(f32[3,64,128]{2,1,0:T(8,128)} %bitcast.11, f32[64,128]{1,0:T(8,128)} %bitcast.12, f32[64,128]{1,0:T(8,128)} %bitcast.8, f32[64,128]{1,0:T(8,128)} %bitcast.13, f32[4,64]{1,0:T(4,128)} %res_hbm.1, s32[1,64]{1,0:T(1,128)} %bitcast.15, ...), custom_call_target="tpu_custom_call" | custom-call | tf_op jit(solution)/shard_map/pallas_call | solution.py:569
  20.6 0.0 copy-start
  20.6 0.0 copy-start.2
  20.7 0.8 %add.9 = f32[64,128]{1,0:T(8,128)S(1)} add(f32[64,128]{1,0:T(8,128)} %get-tuple-element.5, f32[64,128]{1,0:T(8,128)} %get-tuple-element.6) | non-fusion elementwise | flops 8192 | bytes 98304 | tf_op jit(solution)/shard_map/add | solution.py:615
  21.4 0.0 copy-start.1
  21.5 0.0 copy-done
  21.5 0.0 copy-done.2
  21.5 0.6 %multiply_add_fusion = f32[4,16,128]{2,1,0:T(8,128)} fusion(f32[4,16,128]{2,1,0:T(8,128)S(1)} %bitcast.14, f32[4,16,128]{2,1,0:T(8,128)S(1)} %copy-done, f32[4,16,128]{2,1,0:T(8,128)S(1)} %bitcast.9), kind=kLoop, calls=%fused_computation | loop fusion | flops 16384 | bytes 131072 | tf_op jit(solution)/shard_map/add | solution.py:616
  22.1 0.0 copy-done.1
Async XLA Ops:
  20.6 0.8 %copy-start = (f32[4,16,128]{2,1,0:T(8,128)S(1)}, f32[4,16,128]{2,1,0:T(8,128)}, u32[]{:S(2)}) copy-start(f32[4,16,128]{2,1,0:T(8,128)} %param.10) | copy-start | bytes 98308
  20.6 0.8 %copy-start.2 = (f32[64,128]{1,0:T(8,128)S(1)}, f32[64,128]{1,0:T(8,128)}, u32[]{:S(2)}) copy-start(f32[64,128]{1,0:T(8,128)} %get-tuple-element.7) | copy-start | bytes 98308
  21.4 0.6 %copy-start.1 = (f32[64,128]{1,0:T(8,128)}, f32[64,128]{1,0:T(8,128)S(1)}, u32[]{:S(2)}) copy-start(f32[64,128]{1,0:T(8,128)S(1)} %add.9) | copy-start | bytes 98308
